TPU v7x, 256 devices: a whole 4x4x8 slice. The times are simulated.
256 devices in a mesh: space: 64 (over x, z, core), rep: 4 (over y).
Axes of the slice: x: 4, y: 4, z: 8, core: 2. Of those that a mesh axis runs over, the one named last changes fastest.
Arguments:
- voxel_feats: bfloat16 [4, 96, 98304], P('rep', None, 'space'), may hold values from -6 to 6
- kernel_map: int32 [4, 27, 98304], P('rep', None, 'space'), may hold values from 0 to 2304, as said below
- halo_down: int32 [4, 24576], P('rep', 'space'), may hold values from 0 to 1535
- halo_up: int32 [4, 24576], P('rep', 'space'), may hold values from 0 to 1535
- route_slot: int32 [4, 98304], P('rep', 'space'), may hold values from 0 to 1535, as said below
- recv_target: int32 [4, 98304], P('rep', 'space'), may hold values from 0 to 6143, as said below
- subm_weight: bfloat16 [27, 96, 96], replicated, may hold values from -0.125 to 0.125
- down_weight: bfloat16 [8, 96, 192], replicated, may hold values from -0.21875 to 0.21875
- coarse_grad: bfloat16 [4, 192, 49152], P('rep', None, 'space'), may hold values from -0.0134887695 to 0.0134887695
Outputs:
- coarse_feats: bfloat16 [4, 192, 49152], P('rep', None, 'space')
- subm_grad: float32 [27, 96, 96], replicated
- down_grad: float32 [8, 96, 192], replicated
Inputs may be any that keep to these rules, and one draw needn't show every extreme that they name: `kernel_map`: row 27 // 2 (the centre) of a device's block names the voxel itself. Other entries: below 1536 a voxel of the same device; 1536 to 1919 the rows received from the lower neighbour in space, in the order of its halo_up list; the next 384 those from the upper neighbour in the order of its halo_down list; 2304 an absent neighbour. `route_slot`: distinct within a device's block: each device sends exactly 24 rows to every new owner, so every slot is used. `recv_target`: distinct within a device's block; entry s * 24 + j belongs to the row that slot j of device s brings.
All inputs are finite; a program needn't handle non-finite values.
Results may differ from a plain program's by a relative error of at most 0.0053.
Values may be sent and summed in bfloat16 or wider, within the bound.
A program may use at most 128 MiB of HBM per device.

v0:
```python
import jax
import jax.numpy as jnp
from jax import lax
from jax.sharding import PartitionSpec as P


def passed_along(shard, axis, by):
    peers = lax.axis_size(axis)
    pairs = [(i, i + by) for i in range(peers) if 0 <= i + by < peers]
    return lax.ppermute(shard, axis, pairs)


def per_device(
    voxel_feats,
    kernel_map,
    halo_down,
    halo_up,
    route_slot,
    recv_target,
    subm_weight,
    down_weight,
    coarse_grad,
):
    fine_in = voxel_feats[0]
    channels = fine_in.shape[0]
    voxels = fine_in.shape[1]
    offsets = kernel_map.shape[1]
    sent_up = jnp.take(fine_in, halo_up[0], axis=1)
    sent_down = jnp.take(fine_in, halo_down[0], axis=1)
    from_lower = passed_along(sent_up, "space", 1)
    from_upper = passed_along(sent_down, "space", -1)
    stacked = jnp.concatenate(
        [fine_in, from_lower, from_upper, jnp.zeros((channels, 1), jnp.bfloat16)], axis=1
    )
    conv_sum = jnp.zeros((channels, voxels), jnp.float32)
    for offset in range(offsets):
        gathered = jnp.take(stacked, kernel_map[0, offset], axis=1)
        conv_sum = conv_sum + jnp.einsum(
            "io,iv->ov", subm_weight[offset], gathered, preferred_element_type=jnp.float32
        )
    pre_act = fine_in.astype(jnp.float32) + conv_sum
    sigmoid_act = jax.nn.sigmoid(pre_act)
    fine_out = (pre_act * sigmoid_act).astype(jnp.bfloat16)
    slots = recv_target.shape[1]
    children = down_weight.shape[0]
    coarse_count = coarse_grad.shape[2]
    outgoing = jnp.zeros((channels, slots), jnp.bfloat16).at[:, route_slot[0]].set(fine_out)
    received = lax.all_to_all(outgoing, "space", split_axis=1, concat_axis=1, tiled=True)
    cells = (
        jnp.zeros((channels, children * coarse_count), jnp.bfloat16)
        .at[:, recv_target[0]]
        .set(received)
    )
    cells = cells.reshape(channels, children, coarse_count)
    coarse = jnp.einsum(
        "kio,ikc->oc", down_weight, cells, preferred_element_type=jnp.float32
    ).astype(jnp.bfloat16)
    cotangent = coarse_grad[0]
    cell_grad = jnp.einsum(
        "kio,oc->ikc", down_weight, cotangent, preferred_element_type=jnp.float32
    ).astype(jnp.bfloat16)
    cell_grad = cell_grad.reshape(channels, children * coarse_count)
    down_local = jnp.einsum("ikc,oc->kio", cells, cotangent, preferred_element_type=jnp.float32)
    outbound = jnp.take(cell_grad, recv_target[0], axis=1)
    returned = lax.all_to_all(outbound, "space", split_axis=1, concat_axis=1, tiled=True)
    fine_grad = jnp.take(returned, route_slot[0], axis=1)
    pre_grad = (
        fine_grad.astype(jnp.float32) * sigmoid_act * (1.0 + pre_act * (1.0 - sigmoid_act))
    ).astype(jnp.bfloat16)
    grad_terms = []
    for offset in range(offsets):
        gathered = jnp.take(stacked, kernel_map[0, offset], axis=1)
        grad_terms.append(
            jnp.einsum("iv,ov->io", gathered, pre_grad, preferred_element_type=jnp.float32)
        )
    subm_local = jnp.stack(grad_terms)
    subm_total, down_total = lax.psum((subm_local, down_local), ("space", "rep"))
    return (coarse[None], subm_total, down_total)


def solution(mesh):
    in_specs = (
        P("rep", None, "space"),
        P("rep", None, "space"),
        P("rep", "space"),
        P("rep", "space"),
        P("rep", "space"),
        P("rep", "space"),
        P(),
        P(),
        P("rep", None, "space"),
    )
    out_specs = (P("rep", None, "space"), P(), P())
    return jax.shard_map(
        per_device, mesh=mesh, in_specs=in_specs, out_specs=out_specs, check_vma=False
    )
```

profile of v0, /device:TPU:1, one launch (start us, length us, event | category | flops | bytes accessed | tf_op | source)
XLA Modules:
  0.0 512.1 jit_solution(11198102998630706630)
XLA Ops:
  14.9 13.0 %all-to-all-start.1 = ((bf16[96,64,24]{0,2,1:T(8,128)(2,1)}), bf16[96,64,24]{0,2,1:T(8,128)(2,1)S(1)}, u32[]{:S(2)}, u32[]{:S(2)}) async-start(bf16[96,64,24]{0,2,1:T(8,128)(2,1)} %broadcast_select_fusion.27), calls=%async_computation.1 | async-start | bytes 786432 | tf_op jit(solution)/shard_map/all_to_all | solution.py:65
  50.6 4.0 gather_fusion.28
  54.7 4.0 gather_fusion.27
  58.7 4.0 gather_fusion.26
  62.7 4.0 gather_fusion.25
  66.8 4.0 gather_fusion.24
  70.8 4.0 gather_fusion.23
  74.8 4.0 gather_fusion.22
  78.8 4.0 gather_fusion.21
  82.8 4.0 gather_fusion.4
  86.9 4.0 gather_fusion.5
  90.9 4.0 gather_fusion.6
  94.9 4.0 gather_fusion.7
  99.0 4.0 gather_fusion.8
  103.0 4.0 gather_fusion.9
  107.0 4.0 gather_fusion.10
  111.0 4.0 gather_fusion.11
  115.1 4.0 gather_fusion.12
  119.1 4.0 gather_fusion.13
  123.1 4.0 gather_fusion.14
  127.1 4.0 gather_fusion.15
  131.1 4.0 gather_fusion.16
  135.2 4.2 gather_fusion.17
  159.7 4.0 gather_fusion.18
  163.7 4.0 gather_fusion.19
  167.8 4.0 gather_fusion.20
  175.6 4.0 gather_fusion.1
  180.8 4.0 fusion.45
  186.1 5.2 %scatter_custom_fusion = bf16[96,1536]{0,1:T(8,128)(2,1)} fusion(s32[1536]{0:T(1024)S(1)} %fusion.161, bf16[1536,96]{1,0:T(8,128)(2,1)S(1)} %copy.80, bf16[]{:T(256)} %constant.32.clone.1), kind=kCustom, calls=%fused_computation.225 | custom fusion | bytes 294914 | tf_op jit(solution)/shard_map/scatter | solution.py:47
  191.3 10.2 %all-to-all-start = ((bf16[96,64,24]{0,2,1:T(8,128)(2,1)}), bf16[96,64,24]{0,2,1:T(8,128)(2,1)S(1)}, u32[]{:S(2)}, u32[]{:S(2)}) async-start(bf16[96,64,24]{0,2,1:T(8,128)(2,1)} %bitcast.71), calls=%async_computation | async-start | bytes 786432 | tf_op jit(solution)/shard_map/all_to_all | solution.py:48
  233.6 5.0 scatter_custom_fusion.1
  242.5 259.0 %all-reduce.3.cloned.1.call-done = (f32[27,96,96]{2,1,0:T(8,128)}, f32[8,96,192]{2,0,1:T(8,128)}) async-done(((f32[27,96,96]{2,1,0:T(8,128)}, f32[8,96,192]{2,0,1:T(8,128)}), (f32[27,96,96]{2,1,0:T(8,128)}, f32[8,96,192]{2,0,1:T(8,128)})) %all-reduce.3.cloned.1.call-update) | async-done | bytes 1585168 | tf_op jit(solution)/shard_map/psum | solution.py:77
  (333 shorter events, 95.2 us)
Async XLA Ops:
  13.9 14.1 %copy-start.86 = (s32[1,384]{1,0:T(1,128)S(1)}, s32[1,384]{1,0:T(1,128)}, u32[]{:S(2)}) copy-start(s32[1,384]{1,0:T(1,128)} %param.15) | copy-start | bytes 4612
  13.9 14.1 %copy-start.1 = (bf16[1,96,1536]{2,1,0:T(8,128)(2,1)S(1)}, bf16[1,96,1536]{2,1,0:T(8,128)(2,1)}, u32[]{:S(2)}) copy-start(bf16[1,96,1536]{2,1,0:T(8,128)(2,1)} %param.13) | copy-start | bytes 884740
  13.9 14.3 %copy-start.87 = (s32[1,384]{1,0:T(1,128)S(1)}, s32[1,384]{1,0:T(1,128)}, u32[]{:S(2)}) copy-start(s32[1,384]{1,0:T(1,128)} %param.16) | copy-start | bytes 4612
  14.9 160.6 %all-to-all-start.1 = ((bf16[96,64,24]{0,2,1:T(8,128)(2,1)}), bf16[96,64,24]{0,2,1:T(8,128)(2,1)S(1)}, u32[]{:S(2)}, u32[]{:S(2)}) async-start(bf16[96,64,24]{0,2,1:T(8,128)(2,1)} %broadcast_select_fusion.27), calls=%async_computation.1 | async-start | bytes 786432 | tf_op jit(solution)/shard_map/all_to_all | solution.py:65
  28.0 9.6 %copy-start.61 = (s32[1,1536]{1,0:T(1,128)S(1)}, s32[1,1536]{1,0:T(1,128)}, u32[]{:S(2)}) copy-start(s32[1,1536]{1,0:T(1,128)} %param.17) | copy-start | bytes 18436
  28.0 9.6 %copy-start.59 = (s32[1,27,1536]{2,0,1:T(1,128)S(1)}, s32[1,27,1536]{2,0,1:T(1,128)}, u32[]{:S(2)}) copy-start(s32[1,27,1536]{2,0,1:T(1,128)} %param.14) | copy-start | bytes 497668
  29.9 13.9 %collective-permute-start.1 = (bf16[96,384]{1,0:T(8,128)(2,1)S(1)}, bf16[96,384]{1,0:T(8,128)(2,1)S(1)}, u32[]{:S(2)}, u32[]{:S(2)}) collective-permute-start(bf16[96,384]{1,0:T(8,128)(2,1)S(1)} %select_bitcast_fusion), channel_id=1, source_target_pairs={{4,0},{8,4},{12,8},{16,12},{20,16},{24,20},{28,24},{32,28},{36,32}... | collective-permute-start | bytes 221192 | tf_op jit(solution)/shard_map/ppermute | solution.py:10
  33.9 9.9 %collective-permute-start = (bf16[96,384]{1,0:T(8,128)(2,1)S(1)}, bf16[96,384]{1,0:T(8,128)(2,1)S(1)}, u32[]{:S(2)}, u32[]{:S(2)}) collective-permute-start(bf16[96,384]{1,0:T(8,128)(2,1)S(1)} %select_bitcast_fusion.1), channel_id=1, source_target_pairs={{0,4},{4,8},{8,12},{12,16},{16,20},{20,24},{24,28},{28,32},{32,36}... | collective-permute-start | bytes 221192 | tf_op jit(solution)/shard_map/ppermute | solution.py:10
  47.4 92.0 %copy-start.5 = (bf16[1536,96]{1,0:T(8,128)(2,1)}, bf16[1536,96]{1,0:T(8,128)(2,1)S(1)}, u32[]{:S(2)}) copy-start(bf16[1536,96]{1,0:T(8,128)(2,1)S(1)} %gather_fusion.30) | copy-start | bytes 884740
  50.6 90.1 %copy-start.7 = (bf16[1536,96]{1,0:T(8,128)(2,1)}, bf16[1536,96]{1,0:T(8,128)(2,1)S(1)}, u32[]{:S(2)}) copy-start(bf16[1536,96]{1,0:T(8,128)(2,1)S(1)} %gather_fusion.29) | copy-start | bytes 884740
  142.5 3.9 copy-start.17
  143.8 3.9 copy-start.19
  145.1 3.9 copy-start.21
  146.4 3.9 copy-start.51
  146.4 3.9 copy-start.79
  167.8 4.0 copy-start.62
  175.6 5.2 %copy-start.2 = (f32[96,1536]{1,0:T(8,128)S(1)}, f32[96,1536]{1,0:T(8,128)}, u32[]{:S(2)}) copy-start(f32[96,1536]{1,0:T(8,128)} %convolution_bitcast_fusion.3) | copy-start | bytes 1769476
  175.6 5.2 %copy-start.85 = (pred[1536]{0:T(1024)(128)(4,1)S(1)}, pred[1536]{0:T(1024)(128)(4,1)}, u32[]{:S(2)}) copy-start(pred[1536]{0:T(1024)(128)(4,1)} %compare_and_fusion.28) | copy-start | bytes 4612
  184.8 17.0 %copy-start.52 = (bf16[1536,96]{1,0:T(8,128)(2,1)S(1)}, bf16[1536,96]{1,0:T(8,128)(2,1)}, u32[]{:S(2)}) copy-start(bf16[1536,96]{1,0:T(8,128)(2,1)} %gather_fusion.4) | copy-start | bytes 884740
  184.8 17.0 %copy-start.58 = (bf16[96,1536]{1,0:T(8,128)(2,1)S(1)}, bf16[96,1536]{1,0:T(8,128)(2,1)}, u32[]{:S(2)}) copy-start(bf16[96,1536]{1,0:T(8,128)(2,1)} %get-tuple-element.40) | copy-start | bytes 884740
  184.8 17.0 %copy-start.80 = (pred[1536]{0:T(1024)(128)(4,1)S(1)}, pred[1536]{0:T(1024)(128)(4,1)}, u32[]{:S(2)}) copy-start(pred[1536]{0:T(1024)(128)(4,1)} %get-tuple-element.77) | copy-start | bytes 4612
  184.8 18.2 %copy-start.50 = (bf16[1536,96]{1,0:T(8,128)(2,1)S(1)}, bf16[1536,96]{1,0:T(8,128)(2,1)}, u32[]{:S(2)}) copy-start(bf16[1536,96]{1,0:T(8,128)(2,1)} %gather_fusion.5) | copy-start | bytes 884740
  184.8 18.2 %copy-start.74 = (pred[1536]{0:T(1024)(128)(4,1)S(1)}, pred[1536]{0:T(1024)(128)(4,1)}, u32[]{:S(2)}) copy-start(pred[1536]{0:T(1024)(128)(4,1)} %get-tuple-element.76) | copy-start | bytes 4612
  191.3 12.9 %copy-start.48 = (bf16[1536,96]{1,0:T(8,128)(2,1)S(1)}, bf16[1536,96]{1,0:T(8,128)(2,1)}, u32[]{:S(2)}) copy-start(bf16[1536,96]{1,0:T(8,128)(2,1)} %gather_fusion.6) | copy-start | bytes 884740
  191.3 12.9 %copy-start.82 = (pred[1536]{0:T(1024)(128)(4,1)S(1)}, pred[1536]{0:T(1024)(128)(4,1)}, u32[]{:S(2)}) copy-start(pred[1536]{0:T(1024)(128)(4,1)} %get-tuple-element.75) | copy-start | bytes 4612
  191.3 42.3 %all-to-all-start = ((bf16[96,64,24]{0,2,1:T(8,128)(2,1)}), bf16[96,64,24]{0,2,1:T(8,128)(2,1)S(1)}, u32[]{:S(2)}, u32[]{:S(2)}) async-start(bf16[96,64,24]{0,2,1:T(8,128)(2,1)} %bitcast.71), calls=%async_computation | async-start | bytes 786432 | tf_op jit(solution)/shard_map/all_to_all | solution.py:48
  201.5 300.0 %all-reduce.3.cloned.1.call-start = ((), (), s32[]{:S(2)}) async-start(), calls=%async_computation.2 | async-start | bytes 4227072 | tf_op jit(solution)/shard_map/psum | solution.py:77
  201.8 3.6 copy-start.46
  204.2 3.6 copy-start.42
  204.2 3.6 copy-start.70
  205.4 3.6 copy-start.40
  205.4 3.6 copy-start.78
  (61 other events, 146.6 us)
Sparse Core Ops, SparseCore 0:
  241.2 260.2 all-reduce.2
where the time goes:
time: 518 us; the launch traced here: 512 us
  waiting for transfers between devices  259 us (50%)
  local copies, waits for them, and re-layouts  137 us (26%)
  matrix products  63.2 us (12%)
  starting transfers between devices  29.5 us (6%)
  between operations  15.6 us (3%)
  other arithmetic  7.6 us (1%)
    psum x1, waiting for transfers between devices, per_device(): lax.psum((subm_local, down_local), ('space', 'rep'))  259 us
    gather x27, local copies, waits for them, and re-layouts, per_device(): gathered = jnp.take(stacked, kernel_map[0, offset], axis=1)  107 us
    dot_general x27, matrix products, per_device(): jnp.einsum('iv,ov->io', gathered, pre_grad, preferred_element_type=jnp.fl...  31.6 us
    dot_general x27, matrix products, per_device(): jnp.einsum('io,iv->ov', subm_weight[offset], gathered, preferred_element_...  27.4 us
    all_to_all x1, starting transfers between devices, per_device(): lax.all_to_all(outbound, 'space', split_axis=1, concat_axis=1, tiled=True)  13 us
  transfers between devices with their start and end apart: 5, of which 1 were waited for; matrix products, arithmetic and copies ran while one was open for 34% of the time, Pallas kernels for 0%

commit v1 on v0

v1 whole, which is shorter than its diff:
```python
import jax
import jax.numpy as jnp
from jax import lax
from jax.experimental import pallas as pl
from jax.experimental.pallas import tpu as pltpu
from jax.sharding import PartitionSpec as P

C = 96
C2 = 192
OFFSETS = 27
CHILDREN = 8
VOX = 1536
HALO = 384
COARSE = 768
CAP = 24
N_SPACE = 64
N_REP = 4
L = 128
PAD = 32
HALF = (VOX + 2 * HALO) // 2
CHUNK = 256
PEERS_AT_ONCE = 8
MIB = 2**20
MESH = pl.DeviceIdType.MESH
BF = jnp.bfloat16
F32 = jnp.float32

SUBM_TILES = 21
DOWN_TILES = 6
SUBM_SHARE = 64
DOWN_SHARE = 48


def lane_iota(rows):
    return lax.broadcasted_iota(jnp.int32, (rows, L), 1).astype(F32).astype(BF)


def split_index(index):
    top = jnp.floor(index * (1.0 / L))
    return top.astype(BF), (index - L * top).astype(BF)


def onehot(top, low, iota, tiles):
    rows = iota.shape[0]
    zero = jnp.zeros((), BF)
    hit = jnp.where(jnp.broadcast_to(low, (rows, L)) == iota, jnp.ones((), BF), zero)
    tops = jnp.broadcast_to(top, (rows, L))
    return jnp.concatenate(
        [jnp.where(tops == jnp.asarray(t, BF), hit, zero) for t in range(tiles)], axis=1
    )


def onehot_of_row(row, rows):
    spread = jnp.broadcast_to(row, (rows, row.shape[1])).astype(BF)
    iota = lax.broadcasted_iota(jnp.int32, spread.shape, 0).astype(F32).astype(BF)
    return jnp.where(spread == iota, jnp.ones((), BF), jnp.zeros((), BF))


def padded_rows(x, rows):
    return jnp.concatenate([x, jnp.zeros((rows - x.shape[0], x.shape[1]), x.dtype)], axis=0)


def dot(a, b):
    return jnp.dot(a, b, preferred_element_type=F32)


def aligned(i, n):
    return pl.ds(pl.multiple_of(i * n, n), n)


def lanes_of_tile(t):
    q, r = divmod(t, 3)
    first = 4 * q + r
    return ((first, 32 * r, C), (first + 1, 0, 32 * (r + 1)))


def tiles_of_block(k):
    q, r = divmod(k, 4)
    pieces = []
    if r:
        pieces.append((3 * q + r - 1, L - 32 * r, L))
    if r < 3:
        pieces.append((3 * q + r, 0, C - 32 * r))
    return pieces


class Place:
    def __init__(self):
        space, y = lax.axis_index("space"), lax.axis_index("rep")
        core, z, x = space % 2, (space // 2) % 8, space // 16
        at = lambda xx, zz, cc: (xx * 8 + zz) * 2 + cc
        self.space, self.rep, self.core, self.z = space, y, core, z
        self.partner = (at(x, z, 1 - core), y)
        self.plane = [(at((x + d // 4) % 4, z, core), (y + d % 4) % 4) for d in range(16)]
        self.plane_to = [((x + d // 4) % 4) * 4 + (y + d % 4) % 4 for d in range(16)]
        self.plane_from = [((x + 4 - d // 4) % 4) * 4 + (y + 4 - d % 4) % 4 for d in range(16)]
        self.column = [(at(x, (z + d) % 8, core), y) for d in range(8)]
        self.column_from = [(z + 8 - d) % 8 for d in range(8)]


def remote(src, dst, sems, i, peer):
    return pltpu.make_async_remote_copy(
        src_ref=src, dst_ref=dst, send_sem=sems.at[0, i], recv_sem=sems.at[1, i],
        device_id=peer, device_id_type=MESH,
    )


class Reducer:
    @staticmethod
    def scratch(share):
        return [
            pltpu.VMEM((32 * share, L), F32),
            pltpu.VMEM((16 * share, L), BF),
            pltpu.VMEM((16 * share, L), BF),
            pltpu.VMEM((16, share, L), BF),
            pltpu.VMEM((16, share, L), BF),
            pltpu.VMEM((share, L), BF),
            pltpu.VMEM((8, share, L), BF),
            pltpu.VMEM((32 * share, L), BF),
            pltpu.SemaphoreType.DMA((2, 16)),
            pltpu.SemaphoreType.DMA((2, 16)),
            pltpu.SemaphoreType.DMA((2, 8)),
            pltpu.SemaphoreType.DMA((2, 16)),
            pltpu.SemaphoreType.DMA((2, 16)),
        ]

    def __init__(self, place, share, refs):
        self.place, self.share = place, share
        (self.mine, self.theirs, self.pair, self.psend, self.plane, self.zsend, self.column, self.full,
         self.pair_sems, self.plane_sems, self.z_sems, self.back_sems, self.over_sems) = refs
        self.sends = []

    def go(self, copy):
        copy.start()
        self.sends.append(copy)
        return copy

    def start_pair(self):
        p, n = self.place, self.share
        self.theirs[...] = self.mine[aligned(1 - p.core, 16 * n)].astype(BF)
        self.in_pair = []
        for d in range(16):
            at = aligned(p.plane_to[d], n)
            self.in_pair.append(self.go(
                remote(self.theirs.at[at], self.pair.at[at], self.pair_sems, d, p.partner)))

    def start_plane(self):
        p, n = self.place, self.share
        self.in_plane = []
        for d in list(range(1, 16)) + [0]:
            self.in_pair[d].wait_recv()
            both = (self.mine[aligned(p.core * 16 + p.plane_to[d], n)]
                    + self.pair[aligned(p.plane_to[d], n)].astype(F32))
            if d:
                self.psend[d] = both.astype(BF)
                self.in_plane.append(self.go(
                    remote(self.psend.at[d], self.plane.at[d], self.plane_sems, d, p.plane[d])))
        self.total = both

    def start_column(self):
        p = self.place
        total = self.total
        for d in range(1, 16):
            self.in_plane[d - 1].wait_recv()
            total += self.plane[d].astype(F32)
        self.zsend[...] = total.astype(BF)
        self.in_column = []
        for d in range(1, 8):
            self.in_column.append(self.go(
                remote(self.zsend, self.column.at[p.z], self.z_sems, d, p.column[d])))
        self.column[p.z] = total.astype(BF)

    def start_back(self):
        p, n = self.place, self.share
        for copy in self.in_column:
            copy.wait_recv()
        total = self.column[0].astype(F32)
        for z in range(1, 8):
            total += self.column[z].astype(F32)
        here = aligned(p.core * 16 + p.plane_to[0], n)
        self.full[here] = total.astype(BF)
        self.in_back = []
        for d in range(1, 16):
            self.in_back.append(self.go(
                remote(self.full.at[here], self.full.at[here], self.back_sems, d, p.plane[d])))

    def start_over(self):
        p, n = self.place, self.share
        self.in_over = []
        for d in range(16):
            if d:
                self.in_back[d - 1].wait_recv()
            at = aligned(p.core * 16 + p.plane_from[d], n)
            self.in_over.append(self.go(
                remote(self.full.at[at], self.full.at[at], self.over_sems, d, p.partner)))

    def finish(self):
        for copy in self.in_over:
            copy.wait_recv()

    def drain(self):
        for copy in self.sends:
            copy.wait_send()


def pack(block, tiles, count):
    out = []
    for t in range(tiles):
        parts = []
        for k, lo, hi in lanes_of_tile(t):
            if k < count:
                parts.append(block(k, lo, hi))
            else:
                parts.append(jnp.zeros_like(block(0, 0, hi - lo)))
        out.append(jnp.concatenate(parts, axis=1))
    return out


def swap_copy(src, dst, send_sem, recv_sem, peer, me, rep):
    return pltpu.make_async_remote_copy(
        src_ref=src.at[peer], dst_ref=dst.at[me], send_sem=send_sem, recv_sem=recv_sem,
        device_id=(peer, rep), device_id_type=MESH,
    )


def wait_swapped(src, dst, send_sem, recv_sem, me, rep, sent):
    others = pl.ds(0, N_SPACE - 1)
    copies = pltpu.make_async_remote_copy(
        src_ref=src.at[others], dst_ref=dst.at[others], send_sem=send_sem, recv_sem=recv_sem,
        device_id=((me + 1) % N_SPACE, rep), device_id_type=MESH,
    )
    if sent:
        copies.wait_send()
    else:
        copies.wait_recv()


def rows_of_group(ref, group):
    return jnp.concatenate(
        [ref[group * PEERS_AT_ONCE + i].astype(F32)[:CAP] for i in range(PEERS_AT_ONCE)], axis=0
    )


def step_kernel(
    feats_ref, kmap_ref, up_ref, down_ref, route_ref, target_ref, w_ref, wd_ref, cg_ref,
    coarse_ref, sgrad_ref, dgrad_ref,
    own, table, rettab, wpad, wdpad, index, gath, pre_buf, fine, acc, cgt, back, cells_in, dacc,
    hsend, hrecv, bsend, brecv, fsend, frecv, halo_sems, swap_sems, *reduce_refs,
):
    place = Place()
    me, rep = place.space, place.rep
    above, below = (me + 1) % N_SPACE, (me + N_SPACE - 1) % N_SPACE
    barrier = pltpu.get_barrier_semaphore()

    @pl.loop(1, N_SPACE)
    def _(d):
        pl.semaphore_signal(barrier, inc=1, device_id=((me + d) % N_SPACE, rep), device_id_type=MESH)

    others = [place.plane[d] for d in range(16) if d % 4]
    for peer in others:
        pl.semaphore_signal(barrier, inc=1, device_id=peer, device_id_type=MESH)

    own[...] = padded_rows(feats_ref[0].astype(F32), L).T.astype(BF)
    halo_rows = jnp.concatenate([up_ref[...], down_ref[...]], axis=1).astype(F32)
    halo_cols = jnp.broadcast_to(halo_rows, (8, 2 * HALO)).T
    iota_h = lane_iota(HALO)
    for side in range(2):
        top, low = split_index(halo_cols[side * HALO:(side + 1) * HALO, :1])
        hsend[side] = dot(onehot(top, low, iota_h, VOX // L), own[...]).astype(BF)
    to_upper = remote(hsend.at[0], hrecv.at[0], halo_sems, 0, (above, rep))
    to_lower = remote(hsend.at[1], hrecv.at[1], halo_sems, 1, (below, rep))
    pl.semaphore_wait(barrier, N_SPACE - 1 + len(others))
    to_upper.start()
    to_lower.start()

    target = target_ref[...].astype(F32)
    child = jnp.floor((target + 0.5) * (1.0 / COARSE))
    cell = target - COARSE * child
    wdpad[...] = jnp.zeros_like(wdpad)
    for k in range(CHILDREN):
        wdpad[k * L:k * L + C, :C2] = wd_ref[k]
    for block in range(VOX // CHUNK):
        span = slice(block * CHUNK, (block + 1) * CHUNK)
        hits = jnp.concatenate(
            [onehot_of_row(cell[:, span] - b * CHUNK, CHUNK) for b in range(COARSE // CHUNK)], axis=0
        )
        picked = dot(cg_ref[0], hits).astype(BF)
        cgt[:, span] = picked
        every = dot(wdpad[:, :C2], picked)
        chosen = jnp.zeros((L, CHUNK), F32)
        for k in range(CHILDREN):
            chosen = jnp.where(child[:, span] == k, every[k * L:(k + 1) * L], chosen)
        back[span, :] = chosen.T
    for peer in range(N_SPACE):
        bsend[peer] = padded_rows(back[peer * CAP:(peer + 1) * CAP], PAD).astype(BF)
    brecv[me] = bsend[me]

    @pl.loop(1, N_SPACE)
    def _(d):
        swap_copy(bsend, brecv, swap_sems.at[0], swap_sems.at[1], (me + d) % N_SPACE, me, rep).start()

    wpad[...] = jnp.zeros_like(wpad)
    for k in range(OFFSETS):
        wpad[k * L:k * L + C, :C] = w_ref[k]
    rows = jnp.concatenate([kmap_ref[0], route_ref[...]], axis=0).astype(F32)
    index[...] = padded_rows(rows, L).T
    table[:, :L] = own[:HALF]
    table[:VOX - HALF, L:] = own[HALF:]
    to_upper.wait()
    to_lower.wait()
    table[VOX - HALF:VOX - HALF + HALO, L:] = jnp.where(me > 0, hrecv[0], jnp.zeros((), BF))
    table[VOX - HALF + HALO:, L:] = jnp.where(me < N_SPACE - 1, hrecv[1], jnp.zeros((), BF))

    iota_c = lane_iota(CHUNK)

    @pl.loop(0, VOX // CHUNK)
    def _(step):
        here = aligned(step, CHUNK)
        which = index[here, :]
        second = jnp.where(which >= HALF, 1.0, 0.0)
        top, low = split_index(which - HALF * second)
        for k in range(OFFSETS):
            both = dot(onehot(top[:, k:k + 1], low[:, k:k + 1], iota_c, HALF // L), table[...])
            picked = jnp.where(second[:, k:k + 1] > 0.5, both[:, L:], both[:, :L])
            gath[here, k * L:(k + 1) * L] = picked.astype(BF)
        pre = own[here, :].astype(F32) + dot(gath[here, :], wpad[...])
        pre_buf[here, :] = pre
        fine[here, :] = (pre * jax.nn.sigmoid(pre)).astype(BF)

    route = route_ref[...].astype(F32)
    group_rows = PEERS_AT_ONCE * CAP

    @pl.loop(0, N_SPACE // PEERS_AT_ONCE)
    def _(i):
        group = (me // PEERS_AT_ONCE + i) % (N_SPACE // PEERS_AT_ONCE)
        hits = onehot_of_row(route - (group * group_rows).astype(F32), group_rows)
        sent = dot(hits, fine[...])
        for j in range(PEERS_AT_ONCE):
            peer = group * PEERS_AT_ONCE + j
            fsend[peer] = padded_rows(sent[j * CAP:(j + 1) * CAP], PAD).astype(BF)

            @pl.when(peer != me)
            def _():
                swap_copy(fsend, frecv, swap_sems.at[2], swap_sems.at[3], peer, me, rep).start()

    frecv[me] = fsend[me]

    wait_swapped(bsend, brecv, swap_sems.at[0], swap_sems.at[1], me, rep, False)
    groups = N_SPACE // PEERS_AT_ONCE
    for group in range(groups):
        side, at = divmod(group, groups // 2)
        rettab[at * group_rows:(at + 1) * group_rows, side * L:(side + 1) * L] = (
            rows_of_group(brecv, group).astype(BF))
    acc[...] = jnp.zeros_like(acc)

    @pl.loop(0, VOX // CHUNK)
    def _(step):
        here = aligned(step, CHUNK)
        slot = index[here, :][:, OFFSETS:OFFSETS + 1]
        far = jnp.where(slot >= VOX // 2, 1.0, 0.0)
        top, low = split_index(slot - (VOX // 2) * far)
        both = dot(onehot(top, low, iota_c, VOX // 2 // L), rettab[...])
        fine_grad = jnp.where(far > 0.5, both[:, L:], both[:, :L])
        pre = pre_buf[here, :]
        sig = jax.nn.sigmoid(pre)
        pre_grad = fine_grad * sig * (1.0 + pre * (1.0 - sig))
        acc[...] += dot(pre_grad.T.astype(BF), gath[here, :])

    half = len(reduce_refs) // 2
    subm = Reducer(place, SUBM_SHARE, reduce_refs[:half])
    down = Reducer(place, DOWN_SHARE, reduce_refs[half:])
    for t, tile in enumerate(pack(lambda k, lo, hi: acc[:C, k * L + lo:k * L + hi], SUBM_TILES, OFFSETS)):
        subm.mine[t * C:(t + 1) * C] = tile
    subm.mine[SUBM_TILES * C:] = jnp.zeros((32 * SUBM_SHARE - SUBM_TILES * C, L), F32)
    subm.start_pair()
    subm.start_plane()

    wait_swapped(fsend, frecv, swap_sems.at[2], swap_sems.at[3], me, rep, False)
    child_cols = jnp.broadcast_to(child, (8, VOX)).T
    for group in range(groups):
        span = slice(group * group_rows, (group + 1) * group_rows)
        received = rows_of_group(frecv, group)
        kind = jnp.broadcast_to(child_cols[span, :1], (group_rows, L))
        for k in range(CHILDREN):
            cells_in[span, k * L:(k + 1) * L] = jnp.where(kind == k, received, 0.0).astype(BF)
    dacc[...] = dot(cgt[...], cells_in[...])
    for t, tile in enumerate(pack(lambda k, lo, hi: dacc[:, k * L + lo:k * L + hi], DOWN_TILES, CHILDREN)):
        down.mine[t * C2:(t + 1) * C2] = tile
    down.mine[DOWN_TILES * C2:] = jnp.zeros((32 * DOWN_SHARE - DOWN_TILES * C2, L), F32)
    down.start_pair()
    subm.start_column()
    down.start_plane()

    def coarse_block(block):
        hits = onehot_of_row(cell - block * CHUNK, CHUNK)
        cells = dot(hits, cells_in[...]).astype(BF)
        coarse_ref[0, :, block * CHUNK:(block + 1) * CHUNK] = dot(cells, wdpad[...]).T[:C2].astype(BF)

    coarse_block(0)
    subm.start_back()
    down.start_column()
    coarse_block(1)
    subm.start_over()
    down.start_back()
    coarse_block(2)
    down.start_over()
    subm.finish()

    def unpack(full, rows, k):
        parts = [full[t * rows:(t + 1) * rows, lo:hi].astype(F32) for t, lo, hi in tiles_of_block(k)]
        parts.append(jnp.zeros((rows, L - C), F32))
        return jnp.concatenate(parts, axis=1)

    for k in range(OFFSETS):
        sgrad_ref[k] = padded_rows(unpack(subm.full, C, k), L).T[:C, :C]
    down.finish()
    for k in range(CHILDREN):
        dgrad_ref[k] = padded_rows(unpack(down.full, C2, k), 2 * L).T[:C, :C2]
    wait_swapped(bsend, brecv, swap_sems.at[0], swap_sems.at[1], me, rep, True)
    wait_swapped(fsend, frecv, swap_sems.at[2], swap_sems.at[3], me, rep, True)
    subm.drain()
    down.drain()


def per_device(
    voxel_feats, kernel_map, halo_down, halo_up, route_slot, recv_target,
    subm_weight, down_weight, coarse_grad,
):
    vmem = pl.BlockSpec(memory_space=pltpu.VMEM)
    swap = pltpu.VMEM((N_SPACE, PAD, L), BF)
    return pl.pallas_call(
        step_kernel,
        out_shape=(
            jax.ShapeDtypeStruct((1, C2, COARSE), BF),
            jax.ShapeDtypeStruct((OFFSETS, C, C), F32),
            jax.ShapeDtypeStruct((CHILDREN, C, C2), F32),
        ),
        in_specs=[vmem] * 9,
        out_specs=(vmem,) * 3,
        scratch_shapes=[
            pltpu.VMEM((VOX, L), BF),
            pltpu.VMEM((HALF, 2 * L), BF),
            pltpu.VMEM((VOX // 2, 2 * L), BF),
            pltpu.VMEM((OFFSETS * L, L), BF),
            pltpu.VMEM((CHILDREN * L, 2 * L), BF),
            pltpu.VMEM((VOX, L), F32),
            pltpu.VMEM((VOX, OFFSETS * L), BF),
            pltpu.VMEM((VOX, L), F32),
            pltpu.VMEM((VOX, L), BF),
            pltpu.VMEM((L, OFFSETS * L), F32),
            pltpu.VMEM((C2, VOX), BF),
            pltpu.VMEM((VOX, L), F32),
            pltpu.VMEM((VOX, CHILDREN * L), BF),
            pltpu.VMEM((C2, CHILDREN * L), F32),
            pltpu.VMEM((2, HALO, L), BF),
            pltpu.VMEM((2, HALO, L), BF),
            swap, swap, swap, swap,
            pltpu.SemaphoreType.DMA((2, 2)),
            pltpu.SemaphoreType.DMA((4,)),
            *Reducer.scratch(SUBM_SHARE),
            *Reducer.scratch(DOWN_SHARE),
        ],
        compiler_params=pltpu.CompilerParams(
            collective_id=0, has_side_effects=True, vmem_limit_bytes=56 * MIB
        ),
        name="step",
    )(
        voxel_feats, kernel_map, halo_up, halo_down, route_slot, recv_target,
        subm_weight, down_weight, coarse_grad,
    )


def solution(mesh):
    in_specs = (
        P("rep", None, "space"),
        P("rep", None, "space"),
        P("rep", "space"),
        P("rep", "space"),
        P("rep", "space"),
        P("rep", "space"),
        P(),
        P(),
        P("rep", None, "space"),
    )
    out_specs = (P("rep", None, "space"), P(), P())
    return jax.shard_map(
        per_device, mesh=mesh, in_specs=in_specs, out_specs=out_specs, check_vma=False
    )
```

time: 518 us -> 97.8 us (0.19); the launches traced: 512 us -> 97.6 us
  waiting for transfers between devices: 259 us -> 0 us
  local copies, waits for them, and re-layouts: 137 us -> 6.73 us
  Pallas kernels: 0 us -> 90.2 us
  matrix products: 63.2 us -> 0 us
  starting transfers between devices: 29.5 us -> 0 us
  between operations: 15.6 us -> 0.64 us
  other arithmetic: 7.6 us -> 0 us
    psum x1 -> x0, waiting for transfers between devices: 259 us -> none  [per_device(): lax.psum((subm_local, down_local), ('space', 'rep'))]
    gather x34 -> x0, local copies, waits for them, and re-layouts: 119 us -> none  [the longest x27 107 us: per_device(): gathered = jnp.take(stacked, kernel_map[0, offset], axis=1)]
    pallas_call x0 -> x1, Pallas kernels: none -> 90.2 us  [per_device(): pl.pallas_call(step_kernel, out_shape=(jax.ShapeDtypeStruct((1, C2, COARS...]
    dot_general x57 -> x0, matrix products: 63.2 us -> none  [the longest x27 31.6 us: per_device(): jnp.einsum('iv,ov->io', gathered, pre_grad, preferred_element_type=jnp.fl...]
    all_to_all x2 -> x0, starting transfers between devices: 23.2 us -> none  [the longest x1 13 us: per_device(): lax.all_to_all(outbound, 'space', split_axis=1, concat_axis=1, tiled=True)]
    scatter x2 -> x0, local copies, waits for them, and re-layouts: 10.2 us -> none  [the longest x1 5.18 us: per_device(): jnp.zeros((channels, slots), jnp.bfloat16).at[:, route_slot[0]]]
    ppermute x2 -> x0, starting transfers between devices: 6.03 us -> none  [passed_along(): return lax.ppermute(shard, axis, pairs)]
    and x18 -> x0, other arithmetic: 5.35 us -> none  [the longest x14 4.74 us: per_device(): gathered = jnp.take(stacked, kernel_map[0, offset], axis=1)]
  transfers between devices with their start and end apart: 5 -> 0, of which waited for: 1 -> 0; matrix products, arithmetic and copies ran while one was open for 34% -> 0% of each run, Pallas kernels for 0% -> 0%
where the time goes in v1:
time: 97.8 us; the launch traced here: 97.6 us
  Pallas kernels  90.2 us (92%)
  local copies, waits for them, and re-layouts  6.73 us (7%)
    pallas_call x1, Pallas kernels, per_device(): pl.pallas_call(step_kernel, out_shape=(jax.ShapeDtypeStruct((1, C2, COARS...  90.2 us
    unnamed x6, local copies, waits for them, and re-layouts  6.73 us

profile of v1, /device:TPU:1, one launch (start us, length us, event | category | flops | bytes accessed | tf_op | source)
XLA Modules:
  0.0 97.6 jit_solution(13437884022230456103)
XLA Ops:
  0.6 1.6 %copy.12.kmap_ref = s32[1,27,1536]{2,1,0:T(8,128)} copy(s32[1,27,1536]{2,0,1:T(1,128)} %param.10) | data formatting | bytes 331776 | tf_op args[1]
  2.2 90.2 %step.1 = (bf16[1,192,768]{2,1,0:T(8,128)(2,1)}, f32[27,96,96]{2,1,0:T(8,128)}, f32[8,96,192]{2,1,0:T(8,128)}) custom-call(bf16[1,96,1536]{2,1,0:T(8,128)(2,1)} %feats_ref.1, s32[1,27,1536]{2,1,0:T(8,128)} %copy.12.kmap_ref, s32[1,384]{1,0:T(1,128)} %up_ref.1, s32[1,384]{1,0:T(1,128)} %down_ref.1, s32[1,1536]{1,0:T(1,128)} %route_ref.1, ...), custom_call_target="tpu_custom_call" | custom-call | tf_op jit(solution)/shard_map/step/pallas_call | solution.py:431
  92.4 1.7 %copy.16 = bf16[1,192,768]{2,1,0:T(8,128)(2,1)} copy(bf16[1,192,768]{2,1,0:T(8,128)(2,1)} %get-tuple-element.6) | data formatting | bytes 589824
  94.1 0.0 copy-start
  94.1 2.5 %copy.17 = f32[27,96,96]{2,1,0:T(8,128)} copy(f32[27,96,96]{2,1,0:T(8,128)} %get-tuple-element.7) | data formatting | bytes 1990656
  96.7 0.0 copy-done
  96.7 0.9 copy.18
Async XLA Ops:
  94.1 2.5 %copy-start = (f32[8,96,192]{2,1,0:T(8,128)S(1)}, f32[8,96,192]{2,1,0:T(8,128)}, u32[]{:S(2)}) copy-start(f32[8,96,192]{2,1,0:T(8,128)} %get-tuple-element.8) | copy-start | bytes 1769476
